TPU v7x, 512 devices: a whole 4x8x8 slice. The times are simulated.
512 devices in a mesh: fsdp: 64 (over z_lo, y, core), rep: 8 (over z_hi, x).
Axes of the slice: x: 4, y: 8, z: 8 (z_hi: 2, z_lo: 4; z = z_hi * 4 + z_lo), core: 2. Of those that a mesh axis runs over, the one named last changes fastest.
Arguments:
- patches: bfloat16 [131072, 2048], P(('fsdp', 'rep')), may hold values from -24 to 24
- cotangent: bfloat16 [131072, 2048], P(('fsdp', 'rep')), may hold values from -0.015625 to 0.015625
- student: float32 [2048, 2048], P('fsdp'), may hold values from -6 to 6
- first_moment: float32 [2048, 2048], P('fsdp'), may hold values from -4 to 4
- second_moment: float32 [2048, 2048], P('fsdp'), may hold values from 0.0005 to 0.03
- teacher: float32 [2048, 2048], P('fsdp'), may hold values from -6 to 6
Outputs:
- features: bfloat16 [131072, 2048], P(('fsdp', 'rep'))
- new_student: float32 [2048, 2048], P('fsdp')
- new_first: float32 [2048, 2048], P('fsdp')
- new_second: float32 [2048, 2048], P('fsdp')
- new_teacher: float32 [2048, 2048], P('fsdp')
All inputs are finite; a program needn't handle non-finite values.
Results may differ from a plain program's by a relative error of at most 0.006.
Values may be sent and summed in bfloat16 or wider, within the bound.
A program may use at most 128 MiB of HBM per device.

v0:
```python
import jax
import jax.numpy as jnp
from jax import lax
from jax.sharding import PartitionSpec as P

FEAT = 2048
STEP = 100


beta_one = 0.9
beta_two = 0.999
adam_eps = 1e-08
learn_rate = 0.1
decay_rate = 0.04
ema_keep = 0.994


def update_shard(gradient, student, first_moment, second_moment, teacher):
    new_first = beta_one * first_moment + (1.0 - beta_one) * gradient
    new_second = beta_two * second_moment + (1.0 - beta_two) * gradient * gradient
    corr_one = 1.0 - beta_one**STEP
    corr_two = 1.0 - beta_two**STEP
    direction = new_first / corr_one / (jnp.sqrt(new_second / corr_two) + adam_eps)
    new_student = student - learn_rate * (direction + decay_rate * student)
    new_teacher = ema_keep * teacher + (1.0 - ema_keep) * new_student
    return (new_student, new_first, new_second, new_teacher)


def per_device(patches, cotangent, student, first_moment, second_moment, teacher):
    feat_width = patches.shape[1]
    out_width = cotangent.shape[1]
    block_size = min(256, feat_width)
    block_count = feat_width // block_size

    def term_block(index_block):
        columns = lax.dynamic_slice_in_dim(patches, index_block * block_size, block_size, 1)
        return jnp.dot(columns.T, cotangent, preferred_element_type=jnp.float32).astype(
            jnp.bfloat16
        )

    terms = lax.map(term_block, jnp.arange(block_count)).reshape(1, feat_width, out_width)
    group_grad = jnp.sum(
        lax.all_to_all(terms, "fsdp", split_axis=1, concat_axis=0, tiled=True).astype(jnp.float32),
        axis=0,
    )
    columns = patches
    total = jnp.dot(
        columns,
        lax.all_gather(teacher.astype(jnp.bfloat16), "fsdp", axis=0, tiled=True),
        preferred_element_type=jnp.float32,
    )
    gradient = lax.psum(group_grad.astype(jnp.bfloat16), "rep").astype(jnp.float32)
    new_student, new_first, new_second, new_teacher = update_shard(
        gradient, student, first_moment, second_moment, teacher
    )
    features = (total * FEAT ** (-0.5)).astype(jnp.bfloat16)
    return (features, new_student, new_first, new_second, new_teacher)


def solution(mesh):
    placed = (
        P(("fsdp", "rep"), None),
        P(("fsdp", "rep"), None),
        P("fsdp", None),
        P("fsdp", None),
        P("fsdp", None),
        P("fsdp", None),
    )
    return jax.shard_map(
        per_device,
        mesh=mesh,
        in_specs=placed,
        out_specs=(
            P(("fsdp", "rep"), None),
            P("fsdp", None),
            P("fsdp", None),
            P("fsdp", None),
            P("fsdp", None),
        ),
        check_vma=False,
    )
```

profile of v0, /device:TPU:1, one launch (start us, length us, event | category | flops | bytes accessed | tf_op | source)
XLA Modules:
  0.0 631.8 jit_solution(14955053868803481638)
XLA Ops:
  7.2 0.0 all-reduce.2.cloned.1.call-start
  7.2 32.1 %while.10 = (s32[]{:T(128)}, bf16[8,256,2048]{2,1,0:T(8,128)(2,1)}, s32[8]{0:T(128)S(1)}, bf16[256,2048]{1,0:T(8,128)(2,1)}, bf16[256,2048]{1,0:T(8,128)(2,1)}, ...) while((s32[]{:T(128)}, bf16[8,256,2048]{2,1,0:T(8,128)(2,1)}, s32[8]{0:T(128)S(1)}, ...), condition=%wide.region_1.2_spmd, body=%wide.region_0.1_spmd.sunk | while | flops 268959744 | bytes 2228391 | solution.py:41
  7.2 0.6 dynamic_slice.12
  8.5 2.7 fusion.17
  11.2 0.6 dynamic_slice.12
  12.5 2.8 fusion.17
  15.3 0.6 dynamic_slice.12
  16.5 2.8 fusion.17
  19.3 0.6 dynamic_slice.12
  20.5 2.8 fusion.17
  23.3 0.6 dynamic_slice.12
  24.5 2.8 fusion.17
  27.3 0.6 dynamic_slice.12
  28.5 2.8 fusion.17
  31.3 0.6 dynamic_slice.12
  32.5 2.8 fusion.17
  35.3 0.6 dynamic_slice.12
  36.5 2.8 fusion.17
  39.3 15.5 %copy.14 = bf16[1,2048,2048]{2,0,1:T(2,128)(2,1)} copy(bf16[1,2048,2048]{2,1,0:T(8,128)(2,1)} %bitcast.23) | data formatting | bytes 16777216 | tf_op jit(solution)/shard_map/reshape | solution.py:41
  54.8 0.5 broadcast.10
  55.3 51.0 %reduce.3 = bf16[2048,2048]{1,0:T(8,128)(2,1)} reduce(bf16[2048,1,2048]{2,1,0:T(2,128)(2,1)} %bitcast.21, bf16[]{:T(256)} %broadcast.10), dimensions={1}, to_apply=%bitcast.13.reduce_sub_computation | reduce | bytes 16777218
  106.3 14.5 %reshape.19 = bf16[64,2,32768]{2,1,0:T(2,128)(2,1)} reshape(bf16[2048,2048]{1,0:T(8,128)(2,1)} %reduce.3) | data formatting | bytes 16777216
  120.8 200.6 %all_to_all.12 = bf16[64,2,32768]{2,1,0:T(2,128)(2,1)} all-to-all(bf16[64,2,32768]{2,1,0:T(2,128)(2,1)} %reshape.19), channel_id=1, replica_groups=mesh['fsdp'=64,'rep'=8] {'fsdp'}, dimensions={0} | all-to-all | bytes 16777216 | tf_op jit(solution)/shard_map/all_to_all | solution.py:43
  321.4 38.4 %reshape.20 = bf16[2048,1,2048]{2,1,0:T(2,128)(2,1)} reshape(bf16[64,2,32768]{2,1,0:T(2,128)(2,1)} %all_to_all.12) | data formatting | bytes 16777216
  359.8 13.5 %copy.12 = bf16[1,2048,2048]{2,1,0:T(8,128)(2,1)} copy(bf16[1,2048,2048]{2,0,1:T(2,128)(2,1)} %bitcast.20) | data formatting | bytes 16777216
  373.3 0.0 copy-start.1
  373.3 0.0 copy-start.2
  373.3 0.0 copy-start.3
  373.3 0.0 copy-start.4
  373.3 0.0 copy-start
  373.3 5.9 reduce_sum.12
  379.2 0.0 all-reduce.2.cloned.1.call-update
  379.3 0.0 all-gather.2.cloned.1.call-start
  379.3 109.6 %all-reduce.2.cloned.1.call-done = bf16[32,2048]{1,0:T(8,128)(2,1)} async-done(((bf16[32,2048]{1,0:T(8,128)(2,1)}), bf16[32,2048]{1,0:T(8,128)(2,1)}) %all-reduce.2.cloned.1.call-update) | async-done | bytes 131088 | tf_op jit(solution)/shard_map/psum | solution.py:52
  488.9 0.0 copy-done.1
  488.9 0.0 copy-done.2
  488.9 0.0 copy-done.3
  488.9 0.0 copy-done.4
  488.9 2.1 multiply_add_fusion
  491.0 0.0 all-gather.2.cloned.1.call-update
  491.0 127.3 %all-gather.2.cloned.1.call-done = bf16[2048,2048]{1,0:T(8,128)(2,1)} async-done(((bf16[32,2048]{1,0:T(8,128)(2,1)}), bf16[2048,2048]{1,0:T(8,128)(2,1)}) %all-gather.2.cloned.1.call-update) | async-done | bytes 8388624 | tf_op jit(solution)/shard_map/all_gather | solution.py:49
  618.2 0.0 copy-done
  618.3 6.7 %fusion.4 = bf16[256,2048]{1,0:T(8,128)(2,1)} fusion(bf16[256,2048]{1,0:T(8,128)(2,1)S(1)} %copy-done, bf16[2048,2048]{1,0:T(8,128)(2,1)} %all-gather.2.cloned.1.call-done), kind=kOutput, calls=%fused_computation.6 | convolution fusion | flops 2148532224 | bytes 10485760 | tf_op jit(solution)/shard_map/dot_general | solution.py:47
  (2 shorter events, 0.0 us)
Async XLA Ops:
  7.2 481.7 %all-reduce.2.cloned.1.call-start = ((), (), s32[]{:S(2)}) async-start(), calls=%async_computation.2 | async-start | bytes 262144 | tf_op jit(solution)/shard_map/psum | solution.py:52
  373.3 115.6 %copy-start.1 = (f32[32,2048]{1,0:T(8,128)S(1)}, f32[32,2048]{1,0:T(8,128)}, u32[]{:S(2)}) copy-start(f32[32,2048]{1,0:T(8,128)} %param.13) | copy-start | bytes 786436
  373.3 115.6 %copy-start.2 = (f32[32,2048]{1,0:T(8,128)S(1)}, f32[32,2048]{1,0:T(8,128)}, u32[]{:S(2)}) copy-start(f32[32,2048]{1,0:T(8,128)} %param.10) | copy-start | bytes 786436
  373.3 115.6 %copy-start.3 = (f32[32,2048]{1,0:T(8,128)S(1)}, f32[32,2048]{1,0:T(8,128)}, u32[]{:S(2)}) copy-start(f32[32,2048]{1,0:T(8,128)} %param.11) | copy-start | bytes 786436
  373.3 115.6 %copy-start.4 = (f32[32,2048]{1,0:T(8,128)S(1)}, f32[32,2048]{1,0:T(8,128)}, u32[]{:S(2)}) copy-start(f32[32,2048]{1,0:T(8,128)} %param.12) | copy-start | bytes 786436
  373.3 245.0 %copy-start = (bf16[256,2048]{1,0:T(8,128)(2,1)S(1)}, bf16[256,2048]{1,0:T(8,128)(2,1)}, u32[]{:S(2)}) copy-start(bf16[256,2048]{1,0:T(8,128)(2,1)} %get-tuple-element.112) | copy-start | bytes 3145732
  379.3 239.0 %all-gather.2.cloned.1.call-start = ((), (), s32[]{:S(2)}) async-start(), calls=%async_computation.1 | async-start | bytes 8519680 | tf_op jit(solution)/shard_map/all_gather | solution.py:49
Sparse Core Ops, SparseCore 0:
  379.4 109.4 all-reduce.1
  491.8 126.3 all-gather.1
where the time goes:
time: 634 us; the launch traced here: 632 us
  waiting for transfers between devices  237 us (37%)
  blocking collectives  201 us (32%)
  local copies, waits for them, and re-layouts  87 us (14%)
  other arithmetic  59 us (9%)
  matrix products  28.8 us (5%)
  between operations  14.1 us (2%)
    all_to_all x1, blocking collectives, per_device(): lax.all_to_all(terms, 'fsdp', split_axis=1, concat_axis=0, tiled=True)  201 us
    all_gather x1, waiting for transfers between devices, per_device(): lax.all_gather(teacher.astype(jnp.bfloat16), 'fsdp', axis=0, tiled=True)  127 us
    psum x1, waiting for transfers between devices, per_device(): lax.psum(group_grad.astype(jnp.bfloat16), 'rep').astype(jnp.float32)  110 us
    unnamed x14, local copies, waits for them, and re-layouts  66.9 us
    unnamed x1, other arithmetic  51 us
    dot_general x8, matrix products, term_block(): jnp.dot(columns.T, cotangent, preferred_element_type=jnp.float32)  22.1 us
    reshape x1, local copies, waits for them, and re-layouts, per_device(): lax.map(term_block, jnp.arange(block_count))  15.5 us
  transfers between devices with their start and end apart: 2, of which 2 were waited for; matrix products, arithmetic and copies ran while one was open for 0% of the time, Pallas kernels for 0%

commit v1 on v0

v1 whole, which is shorter than its diff:
```python
import jax
import jax.numpy as jnp
from jax import lax
from jax.experimental import pallas as pl
from jax.experimental.pallas import tpu as pltpu
from jax.sharding import PartitionSpec as P

FEAT = 2048
STEP = 100

beta_one = 0.9
beta_two = 0.999
adam_eps = 1e-08
learn_rate = 0.1
decay_rate = 0.04
ema_keep = 0.994

NX, NY, NL, NH = 4, 8, 4, 2
NZ = NL * NH
TOK = 256
HALF = 1024
WA = 384
WB = HALF - WA
XW = 512
MESH = pl.DeviceIdType.MESH
N_SEND = 160
N_RECV = 128
BF = jnp.bfloat16
F32 = jnp.float32


def update_shard(gradient, student, first_moment, second_moment, teacher):
    new_first = beta_one * first_moment + (1.0 - beta_one) * gradient
    new_second = beta_two * second_moment + (1.0 - beta_two) * gradient * gradient
    corr_one = 1.0 - beta_one**STEP
    corr_two = 1.0 - beta_two**STEP
    direction = new_first / corr_one / (jnp.sqrt(new_second / corr_two) + adam_eps)
    new_student = student - learn_rate * (direction + decay_rate * student)
    new_teacher = ema_keep * teacher + (1.0 - ema_keep) * new_student
    return (new_student, new_first, new_second, new_teacher)


def kernel(
    p_ref, c_ref, t_ref,
    feat_ref, grad_ref,
    w, pt, cc, buf_a, buf_b, sum_a, sum_b, got_a, got_b, four_a, four_b, piece, whole,
    send_sem, recv_sem,
):
    fs = lax.axis_index("fsdp")
    rp = lax.axis_index("rep")
    core = lax.rem(fs, 2)
    y = lax.rem(fs // 2, NY)
    zl = fs // (2 * NY)
    zh = rp // NX
    x = lax.rem(rp, NX)
    z = zh * NL + zl
    other = 1 - core

    def dev(x_, y_, z_, c_):
        return ((lax.rem(z_, NL) * NY + y_) * 2 + c_, (z_ // NL) * NX + x_)

    def at_x(d):
        return dev(lax.rem(x + d + NX, NX), y, z, core)

    def at_y(d):
        return dev(x, lax.rem(y + d + NY, NY), z, core)

    def at_z(d):
        return dev(x, y, lax.rem(z + d + NZ, NZ), core)

    sister = dev(x, y, z, other)
    counts = {"s": 0, "r": 0}
    sent = []

    def new_recv():
        counts["r"] += 1
        return counts["r"] - 1

    def send(src, dst, r, to):
        s = counts["s"]
        counts["s"] += 1
        cp = pltpu.make_async_remote_copy(
            src_ref=src, dst_ref=dst, send_sem=send_sem.at[s], recv_sem=recv_sem.at[r],
            device_id=to, device_id_type=MESH,
        )
        cp.start()
        sent.append(cp)

    def wait(dst, r):
        pltpu.make_async_remote_copy(
            src_ref=dst, dst_ref=dst, send_sem=send_sem.at[0], recv_sem=recv_sem.at[r],
            device_id=sister, device_id_type=MESH,
        ).wait_recv()

    barrier = pltpu.get_barrier_semaphore()
    partners = [sister]
    partners += [at_y(d) for d in range(1, NY)]
    partners += [at_z(d) for d in range(1, NZ)]
    partners += [at_x(d) for d in range(1, NX)]
    partners += [dev(x, y, lax.rem(z + NL, NZ), other)]
    for to in partners:
        pl.semaphore_signal(barrier, inc=1, device_id=to, device_id_type=MESH)

    def wblock(xx, yy, cr, lo=0, n=NL):
        return w.at[xx, pl.ds(lo, n), yy, cr]

    def wone(xx, ll, yy, cr):
        return w.at[xx, ll, yy, cr]

    wone(x, zl, y, core)[...] = t_ref[:, pl.ds(pl.multiple_of(x * XW, XW), XW)].astype(BF)
    my_tok = pl.ds(pl.multiple_of(core * TOK, TOK), TOK)
    ot_tok = pl.ds(pl.multiple_of(other * TOK, TOK), TOK)
    for j in range(8):
        pt[j // 2, pl.ds((j % 2) * 4, 4), :, my_tok] = (
            p_ref[:, j * 256:(j + 1) * 256].T.reshape(4, 64, TOK)
        )
    cc[my_tok, :] = c_ref[:, pl.ds(pl.multiple_of(core * HALF, HALF), HALF)]

    pl.semaphore_wait(barrier, len(partners))

    r_c, r_p = new_recv(), new_recv()
    send(c_ref.at[:, pl.ds(pl.multiple_of(other * HALF, HALF), HALF)], cc.at[my_tok, :], r_c, sister)
    send(pt.at[:, :, :, my_tok], pt.at[:, :, :, my_tok], r_p, sister)

    r_z = [new_recv() for _ in range(3)]
    for r, d in zip(r_z, (1, -1, 2)):
        send(wone(x, zl, y, core), wone(x, zl, y, core), r, at_z(d))
    for r, d in zip(r_z, (1, -1, 2)):
        wait(wone(x, lax.rem(zl - d + NL, NL), y, core), r)

    r_sis = [new_recv() for _ in range(NX)]
    r_xr = [new_recv() for _ in range(NY)]
    r_xl = [new_recv() for _ in range(NY)]
    r_opp = [new_recv() for _ in range(NY)]
    r_yr = [new_recv() for _ in range(4)]
    r_yl = [new_recv() for _ in range(4)]
    offs = [0, -1, 1, -2, 2, -3, 3, 4]
    ys = [lax.rem(y + o + NY, NY) for o in offs]
    xs = [x, lax.rem(x - 1 + NX, NX), lax.rem(x + 1, NX), lax.rem(x + 2, NX)]

    def to_sister(k, j):
        send(wblock(xs[k], ys[j], core), wblock(xs[k], ys[j], core), r_sis[k], sister)

    def fan(j):
        b = wblock(x, ys[j], core)
        send(b, b, r_xr[j], at_x(1))
        send(b, b, r_xl[j], at_x(-1))
        to_sister(0, j)

    def y_own():
        b = wblock(x, y, core)
        send(b, b, r_yr[0], at_y(1))
        send(b, b, r_yl[0], at_y(-1))
        fan(0)

    def y_arrive(k):
        if k < 4:
            for o, rs, d, lo in ((-k, r_yr, 1, 0), (k, r_yl, -1, 2)):
                yy = lax.rem(y + o + NY, NY)
                wait(wblock(x, yy, core), rs[k - 1])
                b = wblock(x, yy, core) if k < 3 else wblock(x, yy, core, lo, 2)
                send(b, b, rs[k], at_y(d))
                fan(2 * k - 1 if o < 0 else 2 * k)
        else:
            yy = lax.rem(y + 4, NY)
            wait(wblock(x, yy, core, 0, 2), r_yr[3])
            wait(wblock(x, yy, core, 2, 2), r_yl[3])
            fan(7)

    def x_arrive(j):
        b = wblock(xs[1], ys[j], core)
        wait(b, r_xr[j])
        if j % 2 == 0:
            send(b, b, r_opp[j], at_x(1))
        to_sister(1, j)
        b = wblock(xs[2], ys[j], core)
        wait(b, r_xl[j])
        if j % 2 == 1:
            send(b, b, r_opp[j], at_x(-1))
        to_sister(2, j)

    def opp_arrive(j):
        wait(wblock(xs[3], ys[j], core), r_opp[j])
        to_sister(3, j)

    def features(k):
        xx = xs[k]
        wait(w.at[xx, :, :, other], r_sis[k])
        total = jnp.zeros((TOK, XW), F32)
        for ll in range(NL):
            total += jnp.dot(
                p_ref[:, ll * 512:(ll + 1) * 512],
                w[xx, ll].reshape(512, XW),
                preferred_element_type=F32,
            )
        feat_ref[:, pl.ds(pl.multiple_of(xx * XW, XW), XW)] = (total * FEAT ** (-0.5)).astype(BF)

    def term_a(q, h):
        rows = pt[pl.ds(2 * h, 2), q].reshape(128, 2 * TOK)
        return jnp.dot(rows, cc[:, :WA], preferred_element_type=F32).reshape(2, 64, WA)

    def term_b(q, h):
        rows = pt[
            lax.rem(q, NL), pl.ds(4 * h, 4), pl.ds(pl.multiple_of((q // NL) * 32, 32), 32), :
        ].reshape(128, 2 * TOK)
        return jnp.dot(rows, cc[:, WA:], preferred_element_type=F32).reshape(4, 32, WB)

    streams = [(1, 0, 4), (-1, 1, 4), (1, 1, 3), (-1, 0, 3)]
    slot = {}
    n_slots = 0
    for d, h, length in streams:
        for t in range(length + 1):
            slot[(d, h, t)] = n_slots
            n_slots += 1
    r_ring = {}
    for part in "ab":
        for d, h, length in streams:
            for t in range(1, length + 1):
                r_ring[(part, d, h, t)] = new_recv()

    def ring_step(part, t):
        buf, term, pos, near = (
            (buf_a, term_a, y, at_y) if part == "a" else (buf_b, term_b, z, at_z)
        )
        for d, h, length in streams:
            if t > length:
                continue
            q = lax.rem(pos + d * (length + 1 - t) + 8, 8)
            here = slot[(d, h, t - 1)]
            value = term(q, h)
            if t > 1:
                wait(buf.at[here], r_ring[(part, d, h, t - 1)])
                value = value + buf[here].astype(F32)
            buf[here] = value.astype(BF)
            send(buf.at[here], buf.at[slot[(d, h, t)]], r_ring[(part, d, h, t)], near(d))

    def ring_end(part):
        buf, term, pos = (buf_a, term_a, y) if part == "a" else (buf_b, term_b, z)
        for h in range(2):
            value = term(pos, h)
            for d, hh, length in streams:
                if hh == h:
                    last = slot[(d, h, length)]
                    wait(buf.at[last], r_ring[(part, d, h, length)])
                    value = value + buf[last].astype(F32)
            if part == "a":
                sum_a[pl.ds(2 * h, 2)] = value.reshape(2, NH, 32, WA).astype(BF)
            else:
                sum_b[pl.ds(4 * h, 4)] = value.astype(BF)

    r_da, r_db = new_recv(), new_recv()
    r_xa = [new_recv() for _ in range(3)]
    r_xb = [new_recv() for _ in range(3)]

    def direct_a():
        for d in range(1, NZ):
            zz = lax.rem(z + d, NZ)
            send(sum_a.at[lax.rem(zz, NL), zz // NL], got_a.at[d - 1], r_da, at_z(d))

    def direct_b():
        for d in range(1, NY):
            send(sum_b.at[lax.rem(y + d, NY)], got_b.at[d - 1], r_db, at_y(d))

    def across(part):
        got, four, rd, rx = (
            (got_a, four_a, r_da, r_xa) if part == "a" else (got_b, four_b, r_db, r_xb)
        )
        wait(got, rd)
        value = (sum_a[zl, zh] if part == "a" else sum_b[y]).astype(F32)
        for k in range(7):
            value = value + got[k].astype(F32)
        four[x] = value.astype(BF)
        for d in range(1, NX):
            send(four.at[x], four.at[x], rx[d - 1], at_x(d))

    def finish(part):
        four, rx = (four_a, r_xa) if part == "a" else (four_b, r_xb)
        for d in range(1, NX):
            wait(four.at[lax.rem(x - d + NX, NX)], rx[d - 1])
        value = four[0].astype(F32)
        for k in range(1, NX):
            value = value + four[k].astype(F32)
        if part == "a":
            piece[:, :WA] = value.astype(BF)
        else:
            piece[:, WA:] = value.astype(BF)

    r_far, r_near = new_recv(), new_recv()

    def quad_send():
        send(piece, whole.at[core], r_far, dev(x, y, lax.rem(z + NL, NZ), zh))
        s = counts["s"]
        counts["s"] += 1

        @pl.when(core == zh)
        def _():
            whole[core] = piece[...]

        @pl.when(core != zh)
        def _():
            cp = pltpu.make_async_remote_copy(
                src_ref=piece, dst_ref=whole.at[core], send_sem=send_sem.at[s],
                recv_sem=recv_sem.at[r_near], device_id=sister, device_id_type=MESH,
            )
            cp.start()
            cp.wait_send()

    y_own()
    wait(cc.at[ot_tok, :], r_c)
    wait(pt.at[:, :, :, ot_tok], r_p)
    ring_step("a", 1)
    ring_step("b", 1)
    y_arrive(1)
    y_arrive(2)
    ring_step("a", 2)
    x_arrive(0)
    y_arrive(3)
    ring_step("b", 2)
    y_arrive(4)
    x_arrive(1)
    ring_step("a", 3)
    x_arrive(2)
    ring_step("b", 3)
    ring_step("a", 4)
    x_arrive(3)
    ring_step("b", 4)
    ring_end("a")
    direct_a()
    x_arrive(4)
    opp_arrive(0)
    opp_arrive(1)
    features(0)
    ring_end("b")
    direct_b()
    across("a")
    x_arrive(5)
    opp_arrive(2)
    opp_arrive(3)
    across("b")
    finish("a")
    x_arrive(6)
    opp_arrive(4)
    finish("b")
    quad_send()
    x_arrive(7)
    opp_arrive(5)
    features(1)
    features(2)
    opp_arrive(6)
    opp_arrive(7)

    @pl.when(zh == core)
    def _():
        wait(whole.at[other], r_near)

    @pl.when(zh != core)
    def _():
        wait(whole, r_far)

    grad_ref[:, :HALF] = whole[0]
    grad_ref[:, HALF:] = whole[1]
    features(3)
    for cp in sent:
        cp.wait_send()


def per_device(patches, cotangent, student, first_moment, second_moment, teacher):
    vmem = pl.BlockSpec(memory_space=pltpu.VMEM)
    features, gradient = pl.pallas_call(
        kernel,
        out_shape=(
            jax.ShapeDtypeStruct((TOK, FEAT), BF),
            jax.ShapeDtypeStruct((32, FEAT), BF),
        ),
        in_specs=[vmem] * 3,
        out_specs=(vmem, vmem),
        scratch_shapes=[
            pltpu.VMEM((NX, NL, NY, 2, 32, XW), BF),
            pltpu.VMEM((NL, NY, 64, 2 * TOK), BF),
            pltpu.VMEM((2 * TOK, HALF), BF),
            pltpu.VMEM((18, 2, 64, WA), BF),
            pltpu.VMEM((18, 4, 32, WB), BF),
            pltpu.VMEM((NL, NH, 32, WA), BF),
            pltpu.VMEM((NY, 32, WB), BF),
            pltpu.VMEM((7, 32, WA), BF),
            pltpu.VMEM((7, 32, WB), BF),
            pltpu.VMEM((NX, 32, WA), BF),
            pltpu.VMEM((NX, 32, WB), BF),
            pltpu.VMEM((32, HALF), BF),
            pltpu.VMEM((2, 32, HALF), BF),
            pltpu.SemaphoreType.DMA((N_SEND,)),
            pltpu.SemaphoreType.DMA((N_RECV,)),
        ],
        compiler_params=pltpu.CompilerParams(
            collective_id=0, has_side_effects=True, vmem_limit_bytes=56 * 2**20
        ),
    )(patches, cotangent, teacher)
    new_student, new_first, new_second, new_teacher = update_shard(
        gradient.astype(F32), student, first_moment, second_moment, teacher
    )
    return (features, new_student, new_first, new_second, new_teacher)


def solution(mesh):
    both = P(("fsdp", "rep"), None)
    rows = P("fsdp", None)
    return jax.shard_map(
        per_device,
        mesh=mesh,
        in_specs=(both, both, rows, rows, rows, rows),
        out_specs=(both, rows, rows, rows, rows),
        check_vma=False,
    )
```

time: 634 us -> 85.2 us (0.13)
  waiting for transfers between devices: 237 us -> 0 us
  blocking collectives: 201 us -> 0 us
  local copies, waits for them, and re-layouts: 87 us -> 0.99 us
  Pallas kernels: 0 us -> 81.3 us
  other arithmetic: 59 us -> 2.1 us
  matrix products: 28.8 us -> 0 us
  between operations: 14.1 us -> 0.71 us
    all_to_all x1 -> x0, blocking collectives: 201 us -> none  [per_device(): lax.all_to_all(terms, 'fsdp', split_axis=1, concat_axis=0, tiled=True)]
    all_gather x1 -> x0, waiting for transfers between devices: 127 us -> none  [per_device(): lax.all_gather(teacher.astype(jnp.bfloat16), 'fsdp', axis=0, tiled=True)]
    psum x1 -> x0, waiting for transfers between devices: 110 us -> none  [per_device(): lax.psum(group_grad.astype(jnp.bfloat16), 'rep').astype(jnp.float32)]
    pallas_call x0 -> x1, Pallas kernels: none -> 81.3 us  [per_device(): pl.pallas_call(kernel, out_shape=(jax.ShapeDtypeStruct((TOK, FEAT), BF),...]
    unnamed x14 -> x11, local copies, waits for them, and re-layouts: 66.9 us -> 0.99 us
    unnamed x1 -> x0, other arithmetic: 51 us -> none
    dot_general x9 -> x0, matrix products: 28.8 us -> none  [the longest x8 22.1 us: term_block(): jnp.dot(columns.T, cotangent, preferred_element_type=jnp.float32)]
    reshape x1 -> x0, local copies, waits for them, and re-layouts: 15.5 us -> none  [per_device(): lax.map(term_block, jnp.arange(block_count))]
  transfers between devices with their start and end apart: 2 -> 0, of which waited for: 2 -> 0; matrix products, arithmetic and copies ran while one was open for 0% -> 0% of each run, Pallas kernels for 0% -> 0%
where the time goes in v1:
time: 85.2 us; the launch traced here: 85.1 us
  Pallas kernels  81.3 us (95%)
  other arithmetic  2.1 us (2%)
  local copies, waits for them, and re-layouts  0.99 us (1%)
    pallas_call x1, Pallas kernels, per_device(): pl.pallas_call(kernel, out_shape=(jax.ShapeDtypeStruct((TOK, FEAT), BF),...  81.3 us
    add x1, other arithmetic, update_shard(): new_teacher = ema_keep * teacher + (1.0 - ema_keep) * new_student  2.1 us

profile of v1, /device:TPU:1, one launch (start us, length us, event | category | flops | bytes accessed | tf_op | source)
XLA Modules:
  0.0 85.1 jit_solution(15037574195408836674)
XLA Ops:
  0.6 0.0 copy-start
  0.6 0.0 copy-start.4
  0.7 0.0 copy-start.3
  0.7 0.0 copy-start.2
  0.7 81.3 %shard_map.101 = (bf16[256,2048]{1,0:T(8,128)(2,1)}, bf16[32,2048]{1,0:T(8,128)(2,1)}) custom-call(bf16[256,2048]{1,0:T(8,128)(2,1)} %p_ref.1, bf16[256,2048]{1,0:T(8,128)(2,1)} %c_ref.1, f32[32,2048]{1,0:T(8,128)} %t_ref.1), custom_call_target="tpu_custom_call" | custom-call | tf_op jit(solution)/shard_map/pallas_call | solution.py:369
  82.0 0.0 copy-done
  82.0 0.0 copy-done.4
  82.0 0.0 copy-done.3
  82.0 0.0 copy-done.2
  82.0 0.0 copy-start.1
  82.0 2.1 %multiply_add_fusion = (f32[32,2048]{1,0:T(8,128)}, f32[32,2048]{1,0:T(8,128)}, f32[32,2048]{1,0:T(8,128)}, f32[32,2048]{1,0:T(8,128)}) fusion(f32[32,2048]{1,0:T(8,128)S(1)} %copy-done, f32[32,2048]{1,0:T(8,128)S(1)} %copy-done.2, bf16[32,2048]{1,0:T(8,128)(2,1)} %get-tuple-element.8, f32[32,2048]{1,0:T(8,128)S(1)} %copy-done.3, f32[32,2048]{1,0:T(8,128)S(1)} %copy-done.4), kind=kLoop, calls=%fused_computation.4 | loop fusion | flops 1245184 | bytes 2228224 | tf_op jit(solution)/shard_map/add | solution.py:39
  84.1 0.0 copy-done.1
  84.1 1.0 %copy.12 = bf16[256,2048]{1,0:T(8,128)(2,1)} copy(bf16[256,2048]{1,0:T(8,128)(2,1)S(1)} %copy-done.1) | data formatting | bytes 2097152
Async XLA Ops:
  0.6 81.3 %copy-start = (f32[32,2048]{1,0:T(8,128)S(1)}, f32[32,2048]{1,0:T(8,128)}, u32[]{:S(2)}) copy-start(f32[32,2048]{1,0:T(8,128)} %t_ref.1) | copy-start | bytes 786436
  0.6 81.3 %copy-start.4 = (f32[32,2048]{1,0:T(8,128)S(1)}, f32[32,2048]{1,0:T(8,128)}, u32[]{:S(2)}) copy-start(f32[32,2048]{1,0:T(8,128)} %param.10) | copy-start | bytes 786436
  0.7 81.3 %copy-start.3 = (f32[32,2048]{1,0:T(8,128)S(1)}, f32[32,2048]{1,0:T(8,128)}, u32[]{:S(2)}) copy-start(f32[32,2048]{1,0:T(8,128)} %param.9) | copy-start | bytes 786436
  0.7 81.3 %copy-start.2 = (f32[32,2048]{1,0:T(8,128)S(1)}, f32[32,2048]{1,0:T(8,128)}, u32[]{:S(2)}) copy-start(f32[32,2048]{1,0:T(8,128)} %param.8) | copy-start | bytes 786436
  82.0 2.1 %copy-start.1 = (bf16[256,2048]{1,0:T(8,128)(2,1)S(1)}, bf16[256,2048]{1,0:T(8,128)(2,1)}, u32[]{:S(2)}) copy-start(bf16[256,2048]{1,0:T(8,128)(2,1)} %get-tuple-element.18) | copy-start | bytes 3145732

commit v2 on v1

--- a/solution.py
+++ b/solution.py
@@ -19,7 +19,7 @@
 NZ = NL * NH
 TOK = 256
 HALF = 1024
-WA = 384
+WA = 512
 WB = HALF - WA
 XW = 512
 MESH = pl.DeviceIdType.MESH
@@ -43,8 +43,8 @@
 def kernel(
     p_ref, c_ref, t_ref,
     feat_ref, grad_ref,
-    w, pt, cc, buf_a, buf_b, sum_a, sum_b, got_a, got_b, four_a, four_b, piece, whole,
-    send_sem, recv_sem,
+    p_v, t_v, feat_v, w, pt, cc, buf_a, buf_b, sum_a, sum_b, got_a, got_b, four_a, four_b, piece_a, piece_b, whole_a, whole_b,
+    load_sem, send_sem, recv_sem,
 ):
     fs = lax.axis_index("fsdp")
     rp = lax.axis_index("rep")
@@ -107,24 +107,45 @@
     def wone(xx, ll, yy, cr):
         return w.at[xx, ll, yy, cr]
 
-    wone(x, zl, y, core)[...] = t_ref[:, pl.ds(pl.multiple_of(x * XW, XW), XW)].astype(BF)
     my_tok = pl.ds(pl.multiple_of(core * TOK, TOK), TOK)
     ot_tok = pl.ds(pl.multiple_of(other * TOK, TOK), TOK)
-    for j in range(8):
-        pt[j // 2, pl.ds((j % 2) * 4, 4), :, my_tok] = (
-            p_ref[:, j * 256:(j + 1) * 256].T.reshape(4, 64, TOK)
-        )
-    cc[my_tok, :] = c_ref[:, pl.ds(pl.multiple_of(core * HALF, HALF), HALF)]
-
+    loads = [
+        pltpu.make_async_copy(
+            t_ref.at[:, pl.ds(pl.multiple_of(x * XW, XW), XW)], t_v, load_sem.at[0]
+        ),
+        pltpu.make_async_copy(p_ref, p_v, load_sem.at[1]),
+        pltpu.make_async_copy(
+            c_ref.at[:, pl.ds(pl.multiple_of(core * HALF, HALF), HALF)],
+            cc.at[my_tok, :], load_sem.at[2],
+        ),
+    ]
+    for cp in loads:
+        cp.start()
+    loads[0].wait()
+    wone(x, zl, y, core)[...] = t_v[...].astype(BF)
+    loads[1].wait()
+
+    def turn(ll):
+        for j in (2 * ll, 2 * ll + 1):
+            pt[ll, pl.ds((j % 2) * 4, 4), :, my_tok] = (
+                p_v[:, j * 256:(j + 1) * 256].T.reshape(4, 64, TOK)
+            )
+
+    turn(0)
     pl.semaphore_wait(barrier, len(partners))
 
-    r_c, r_p = new_recv(), new_recv()
-    send(c_ref.at[:, pl.ds(pl.multiple_of(other * HALF, HALF), HALF)], cc.at[my_tok, :], r_c, sister)
-    send(pt.at[:, :, :, my_tok], pt.at[:, :, :, my_tok], r_p, sister)
-
+    r_c = new_recv()
+    r_p = [new_recv() for _ in range(NL)]
     r_z = [new_recv() for _ in range(3)]
     for r, d in zip(r_z, (1, -1, 2)):
         send(wone(x, zl, y, core), wone(x, zl, y, core), r, at_z(d))
+    send(c_ref.at[:, pl.ds(pl.multiple_of(other * HALF, HALF), HALF)], cc.at[my_tok, :], r_c, sister)
+    for ll in range(NL):
+        if ll:
+            turn(ll)
+        send(pt.at[ll, :, :, my_tok], pt.at[ll, :, :, my_tok], r_p[ll], sister)
+    loads[2].wait()
+
     for r, d in zip(r_z, (1, -1, 2)):
         wait(wone(x, lax.rem(zl - d + NL, NL), y, core), r)
 
@@ -153,31 +174,27 @@
         send(b, b, r_yl[0], at_y(-1))
         fan(0)
 
-    def y_arrive(k):
-        if k < 4:
-            for o, rs, d, lo in ((-k, r_yr, 1, 0), (k, r_yl, -1, 2)):
-                yy = lax.rem(y + o + NY, NY)
-                wait(wblock(x, yy, core), rs[k - 1])
-                b = wblock(x, yy, core) if k < 3 else wblock(x, yy, core, lo, 2)
-                send(b, b, rs[k], at_y(d))
-                fan(2 * k - 1 if o < 0 else 2 * k)
-        else:
-            yy = lax.rem(y + 4, NY)
-            wait(wblock(x, yy, core, 0, 2), r_yr[3])
-            wait(wblock(x, yy, core, 2, 2), r_yl[3])
-            fan(7)
-
-    def x_arrive(j):
-        b = wblock(xs[1], ys[j], core)
-        wait(b, r_xr[j])
-        if j % 2 == 0:
-            send(b, b, r_opp[j], at_x(1))
-        to_sister(1, j)
-        b = wblock(xs[2], ys[j], core)
-        wait(b, r_xl[j])
-        if j % 2 == 1:
-            send(b, b, r_opp[j], at_x(-1))
-        to_sister(2, j)
+    def y_from(side, k):
+        o, rs, d, lo = ((-k, r_yr, 1, 0), (k, r_yl, -1, 2))[side]
+        yy = lax.rem(y + o + NY, NY)
+        wait(wblock(x, yy, core), rs[k - 1])
+        b = wblock(x, yy, core) if k < 3 else wblock(x, yy, core, lo, 2)
+        send(b, b, rs[k], at_y(d))
+        fan(2 * k - 1 if o < 0 else 2 * k)
+
+    def y_last():
+        yy = lax.rem(y + 4, NY)
+        wait(wblock(x, yy, core, 0, 2), r_yr[3])
+        wait(wblock(x, yy, core, 2, 2), r_yl[3])
+        fan(7)
+
+    def x_from(side, j):
+        rs, d = ((r_xr, 1), (r_xl, -1))[side]
+        b = wblock(xs[1 + side], ys[j], core)
+        wait(b, rs[j])
+        if j % 2 == side:
+            send(b, b, r_opp[j], at_x(d))
+        to_sister(1 + side, j)
 
     def opp_arrive(j):
         wait(wblock(xs[3], ys[j], core), r_opp[j])
@@ -189,11 +206,16 @@
         total = jnp.zeros((TOK, XW), F32)
         for ll in range(NL):
             total += jnp.dot(
-                p_ref[:, ll * 512:(ll + 1) * 512],
+                p_v[:, ll * 512:(ll + 1) * 512],
                 w[xx, ll].reshape(512, XW),
                 preferred_element_type=F32,
             )
-        feat_ref[:, pl.ds(pl.multiple_of(xx * XW, XW), XW)] = (total * FEAT ** (-0.5)).astype(BF)
+        feat_v[k] = (total * FEAT ** (-0.5)).astype(BF)
+        feat_copy(k).start()
+
+    def feat_copy(k):
+        cols = pl.ds(pl.multiple_of(xs[k] * XW, XW), XW)
+        return pltpu.make_async_copy(feat_v.at[k], feat_ref.at[:, cols], load_sem.at[3 + k])
 
     def term_a(q, h):
         rows = pt[pl.ds(2 * h, 2), q].reshape(128, 2 * TOK)
@@ -218,40 +240,34 @@
             for t in range(1, length + 1):
                 r_ring[(part, d, h, t)] = new_recv()
 
-    def ring_step(part, t):
+    def ring_step(part, i, t):
         buf, term, pos, near = (
             (buf_a, term_a, y, at_y) if part == "a" else (buf_b, term_b, z, at_z)
         )
-        for d, h, length in streams:
-            if t > length:
-                continue
-            q = lax.rem(pos + d * (length + 1 - t) + 8, 8)
-            here = slot[(d, h, t - 1)]
-            value = term(q, h)
-            if t > 1:
-                wait(buf.at[here], r_ring[(part, d, h, t - 1)])
-                value = value + buf[here].astype(F32)
-            buf[here] = value.astype(BF)
-            send(buf.at[here], buf.at[slot[(d, h, t)]], r_ring[(part, d, h, t)], near(d))
-
-    def ring_end(part):
+        d, h, length = streams[i]
+        q = lax.rem(pos + d * (length + 1 - t) + 8, 8)
+        here = slot[(d, h, t - 1)]
+        value = term(q, h)
+        if t > 1:
+            wait(buf.at[here], r_ring[(part, d, h, t - 1)])
+            value = value + buf[here].astype(F32)
+        buf[here] = value.astype(BF)
+        send(buf.at[here], buf.at[slot[(d, h, t)]], r_ring[(part, d, h, t)], near(d))
+
+    def ring_end(part, h):
         buf, term, pos = (buf_a, term_a, y) if part == "a" else (buf_b, term_b, z)
-        for h in range(2):
-            value = term(pos, h)
-            for d, hh, length in streams:
-                if hh == h:
-                    last = slot[(d, h, length)]
-                    wait(buf.at[last], r_ring[(part, d, h, length)])
-                    value = value + buf[last].astype(F32)
-            if part == "a":
-                sum_a[pl.ds(2 * h, 2)] = value.reshape(2, NH, 32, WA).astype(BF)
-            else:
-                sum_b[pl.ds(4 * h, 4)] = value.astype(BF)
+        value = term(pos, h)
+        for d, hh, length in streams:
+            if hh == h:
+                last = slot[(d, h, length)]
+                wait(buf.at[last], r_ring[(part, d, h, length)])
+                value = value + buf[last].astype(F32)
+        if part == "a":
+            sum_a[pl.ds(2 * h, 2)] = value.reshape(2, NH, 32, WA).astype(BF)
+        else:
+            sum_b[pl.ds(4 * h, 4)] = value.astype(BF)
 
     r_da, r_db = new_recv(), new_recv()
-    r_xa = [new_recv() for _ in range(3)]
-    r_xb = [new_recv() for _ in range(3)]
-
     def direct_a():
         for d in range(1, NZ):
             zz = lax.rem(z + d, NZ)
@@ -261,34 +277,29 @@
         for d in range(1, NY):
             send(sum_b.at[lax.rem(y + d, NY)], got_b.at[d - 1], r_db, at_y(d))
 
+    r_x = {part: [new_recv() for _ in range(3)] for part in "ab"}
+    r_far = {part: new_recv() for part in "ab"}
+    r_near = {part: new_recv() for part in "ab"}
+
     def across(part):
-        got, four, rd, rx = (
-            (got_a, four_a, r_da, r_xa) if part == "a" else (got_b, four_b, r_db, r_xb)
-        )
+        got, four, rd = (got_a, four_a, r_da) if part == "a" else (got_b, four_b, r_db)
         wait(got, rd)
         value = (sum_a[zl, zh] if part == "a" else sum_b[y]).astype(F32)
         for k in range(7):
             value = value + got[k].astype(F32)
         four[x] = value.astype(BF)
         for d in range(1, NX):
-            send(four.at[x], four.at[x], rx[d - 1], at_x(d))
-
-    def finish(part):
-        four, rx = (four_a, r_xa) if part == "a" else (four_b, r_xb)
+            send(four.at[x], four.at[x], r_x[part][d - 1], at_x(d))
+
+    def quad(part):
+        four, piece, whole = (four_a, piece_a, whole_a) if part == "a" else (four_b, piece_b, whole_b)
         for d in range(1, NX):
-            wait(four.at[lax.rem(x - d + NX, NX)], rx[d - 1])
+            wait(four.at[lax.rem(x - d + NX, NX)], r_x[part][d - 1])
         value = four[0].astype(F32)
         for k in range(1, NX):
             value = value + four[k].astype(F32)
-        if part == "a":
-            piece[:, :WA] = value.astype(BF)
-        else:
-            piece[:, WA:] = value.astype(BF)
-
-    r_far, r_near = new_recv(), new_recv()
-
-    def quad_send():
-        send(piece, whole.at[core], r_far, dev(x, y, lax.rem(z + NL, NZ), zh))
+        piece[...] = value.astype(BF)
+        send(piece, whole.at[core], r_far[part], dev(x, y, lax.rem(z + NL, NZ), zh))
         s = counts["s"]
         counts["s"] += 1
 
@@ -300,81 +311,125 @@
         def _():
             cp = pltpu.make_async_remote_copy(
                 src_ref=piece, dst_ref=whole.at[core], send_sem=send_sem.at[s],
-                recv_sem=recv_sem.at[r_near], device_id=sister, device_id_type=MESH,
+                recv_sem=recv_sem.at[r_near[part]], device_id=sister, device_id_type=MESH,
             )
             cp.start()
             cp.wait_send()
 
+    def collect(part):
+        whole, lo, n = (whole_a, 0, WA) if part == "a" else (whole_b, WA, WB)
+
+        @pl.when(zh == core)
+        def _():
+            wait(whole.at[other], r_near[part])
+
+        @pl.when(zh != core)
+        def _():
+            wait(whole, r_far[part])
+
+        for cr in range(2):
+            grad_ref[:, cr * HALF + lo:cr * HALF + lo + n] = whole[cr]
+
     y_own()
     wait(cc.at[ot_tok, :], r_c)
-    wait(pt.at[:, :, :, ot_tok], r_p)
-    ring_step("a", 1)
-    ring_step("b", 1)
-    y_arrive(1)
-    y_arrive(2)
-    ring_step("a", 2)
-    x_arrive(0)
-    y_arrive(3)
-    ring_step("b", 2)
-    y_arrive(4)
-    x_arrive(1)
-    ring_step("a", 3)
-    x_arrive(2)
-    ring_step("b", 3)
-    ring_step("a", 4)
-    x_arrive(3)
-    ring_step("b", 4)
-    ring_end("a")
+    for ll in range(NL):
+        wait(pt.at[ll, :, :, ot_tok], r_p[ll])
+    ring_step("a", 0, 1)
+    ring_step("a", 1, 1)
+    ring_step("b", 1, 1)
+    y_from(0, 1)
+    ring_step("b", 0, 1)
+    ring_step("a", 3, 1)
+    ring_step("b", 3, 1)
+    ring_step("b", 2, 1)
+    ring_step("a", 0, 2)
+    y_from(1, 1)
+    ring_step("b", 1, 2)
+    ring_step("b", 0, 2)
+    ring_step("a", 1, 2)
+    y_from(0, 2)
+    ring_step("a", 2, 1)
+    ring_step("b", 2, 2)
+    ring_step("b", 3, 2)
+    ring_step("a", 0, 3)
+    y_from(1, 2)
+    ring_step("b", 1, 3)
+    ring_step("b", 0, 3)
+    y_from(0, 3)
+    x_from(0, 2)
+    x_from(0, 3)
+    ring_step("a", 3, 2)
+    x_from(1, 1)
+    ring_step("a", 2, 2)
+    ring_step("b", 2, 3)
+    x_from(0, 0)
+    x_from(1, 2)
+    ring_step("a", 1, 3)
+    ring_step("b", 3, 3)
+    ring_step("b", 0, 4)
+    ring_step("a", 3, 3)
+    ring_step("a", 0, 4)
+    ring_step("b", 1, 4)
+    ring_step("a", 1, 4)
+    x_from(1, 3)
+    opp_arrive(2)
+    ring_step("a", 2, 3)
+    y_from(1, 3)
+    x_from(0, 4)
+    ring_end("b", 0)
+    ring_end("b", 1)
+    direct_b()
+    ring_end("a", 0)
+    ring_end("a", 1)
     direct_a()
-    x_arrive(4)
+    x_from(1, 5)
+    x_from(0, 1)
+    y_last()
+    x_from(0, 6)
+    features(0)
+    x_from(1, 6)
+    x_from(1, 4)
+    across("b")
+    opp_arrive(1)
+    x_from(0, 5)
+    x_from(0, 7)
+    across("a")
+    x_from(1, 7)
     opp_arrive(0)
-    opp_arrive(1)
-    features(0)
-    ring_end("b")
-    direct_b()
-    across("a")
-    x_arrive(5)
-    opp_arrive(2)
-    opp_arrive(3)
-    across("b")
-    finish("a")
-    x_arrive(6)
-    opp_arrive(4)
-    finish("b")
-    quad_send()
-    x_arrive(7)
+    quad("b")
+    opp_arrive(6)
     opp_arrive(5)
     features(1)
+    quad("a")
+    opp_arrive(3)
+    x_from(1, 0)
+    opp_arrive(4)
+    opp_arrive(7)
     features(2)
-    opp_arrive(6)
-    opp_arrive(7)
-
-    @pl.when(zh == core)
-    def _():
-        wait(whole.at[other], r_near)
-
-    @pl.when(zh != core)
-    def _():
-        wait(whole, r_far)
-
-    grad_ref[:, :HALF] = whole[0]
-    grad_ref[:, HALF:] = whole[1]
     features(3)
+    collect("b")
+    collect("a")
+    for k in range(NX):
+        feat_copy(k).wait()
     for cp in sent:
         cp.wait_send()
 
 
 def per_device(patches, cotangent, student, first_moment, second_moment, teacher):
     vmem = pl.BlockSpec(memory_space=pltpu.VMEM)
+    hbm = pl.BlockSpec(memory_space=pl.ANY)
     features, gradient = pl.pallas_call(
         kernel,
         out_shape=(
             jax.ShapeDtypeStruct((TOK, FEAT), BF),
             jax.ShapeDtypeStruct((32, FEAT), BF),
         ),
-        in_specs=[vmem] * 3,
-        out_specs=(vmem, vmem),
+        in_specs=[hbm] * 3,
+        out_specs=(hbm, vmem),
         scratch_shapes=[
+            pltpu.VMEM((TOK, FEAT), BF),
+            pltpu.VMEM((32, XW), F32),
+            pltpu.VMEM((NX, TOK, XW), BF),
             pltpu.VMEM((NX, NL, NY, 2, 32, XW), BF),
             pltpu.VMEM((NL, NY, 64, 2 * TOK), BF),
             pltpu.VMEM((2 * TOK, HALF), BF),
@@ -386,8 +441,11 @@
             pltpu.VMEM((7, 32, WB), BF),
             pltpu.VMEM((NX, 32, WA), BF),
             pltpu.VMEM((NX, 32, WB), BF),
-            pltpu.VMEM((32, HALF), BF),
-            pltpu.VMEM((2, 32, HALF), BF),
+            pltpu.VMEM((32, WA), BF),
+            pltpu.VMEM((32, WB), BF),
+            pltpu.VMEM((2, 32, WA), BF),
+            pltpu.VMEM((2, 32, WB), BF),
+            pltpu.SemaphoreType.DMA((3 + NX,)),
             pltpu.SemaphoreType.DMA((N_SEND,)),
             pltpu.SemaphoreType.DMA((N_RECV,)),
         ],

time: 85.2 us -> 77 us (0.904)
  Pallas kernels: 81.3 us -> 73 us
    pallas_call x1, Pallas kernels: 81.3 us -> 73 us  [per_device(): pl.pallas_call(kernel, out_shape=(jax.ShapeDtypeStruct((TOK, FEAT), BF),...]
where the time goes in v2:
time: 77 us; the launch traced here: 76.8 us
  Pallas kernels  73 us (95%)
  other arithmetic  2.1 us (3%)
  local copies, waits for them, and re-layouts  0.99 us (1%)
    pallas_call x1, Pallas kernels, per_device(): pl.pallas_call(kernel, out_shape=(jax.ShapeDtypeStruct((TOK, FEAT), BF),...  73 us
    add x1, other arithmetic, update_shard(): new_teacher = ema_keep * teacher + (1.0 - ema_keep) * new_student  2.1 us

profile of v2, /device:TPU:1, one launch (start us, length us, event | category | flops | bytes accessed | tf_op | source)
XLA Modules:
  0.0 76.8 jit_solution(10800996752116243672)
XLA Ops:
  0.6 0.0 copy-start
  0.6 0.0 copy-start.4
  0.7 0.0 copy-start.3
  0.7 0.0 copy-start.2
  0.7 73.0 %shard_map.101 = (bf16[256,2048]{1,0:T(8,128)(2,1)}, bf16[32,2048]{1,0:T(8,128)(2,1)}) custom-call(bf16[256,2048]{1,0:T(8,128)(2,1)} %p_ref.1, bf16[256,2048]{1,0:T(8,128)(2,1)} %c_ref.1, f32[32,2048]{1,0:T(8,128)} %t_ref.1), custom_call_target="tpu_custom_call" | custom-call | tf_op jit(solution)/shard_map/pallas_call | solution.py:421
  73.7 0.0 copy-done
  73.7 0.0 copy-done.4
  73.7 0.0 copy-done.3
  73.7 0.0 copy-done.2
  73.8 0.0 copy-start.1
  73.8 2.1 %multiply_add_fusion = (f32[32,2048]{1,0:T(8,128)}, f32[32,2048]{1,0:T(8,128)}, f32[32,2048]{1,0:T(8,128)}, f32[32,2048]{1,0:T(8,128)}) fusion(f32[32,2048]{1,0:T(8,128)S(1)} %copy-done, f32[32,2048]{1,0:T(8,128)S(1)} %copy-done.2, bf16[32,2048]{1,0:T(8,128)(2,1)} %get-tuple-element.8, f32[32,2048]{1,0:T(8,128)S(1)} %copy-done.3, f32[32,2048]{1,0:T(8,128)S(1)} %copy-done.4), kind=kLoop, calls=%fused_computation.4 | loop fusion | flops 1245184 | bytes 2228224 | tf_op jit(solution)/shard_map/add | solution.py:39
  75.9 0.0 copy-done.1
  75.9 1.0 %copy.12 = bf16[256,2048]{1,0:T(8,128)(2,1)} copy(bf16[256,2048]{1,0:T(8,128)(2,1)S(1)} %copy-done.1) | data formatting | bytes 2097152
Async XLA Ops:
  0.6 73.1 %copy-start = (f32[32,2048]{1,0:T(8,128)S(1)}, f32[32,2048]{1,0:T(8,128)}, u32[]{:S(2)}) copy-start(f32[32,2048]{1,0:T(8,128)} %t_ref.1) | copy-start | bytes 786436
  0.6 73.1 %copy-start.4 = (f32[32,2048]{1,0:T(8,128)S(1)}, f32[32,2048]{1,0:T(8,128)}, u32[]{:S(2)}) copy-start(f32[32,2048]{1,0:T(8,128)} %param.10) | copy-start | bytes 786436
  0.7 73.1 %copy-start.3 = (f32[32,2048]{1,0:T(8,128)S(1)}, f32[32,2048]{1,0:T(8,128)}, u32[]{:S(2)}) copy-start(f32[32,2048]{1,0:T(8,128)} %param.9) | copy-start | bytes 786436
  0.7 73.1 %copy-start.2 = (f32[32,2048]{1,0:T(8,128)S(1)}, f32[32,2048]{1,0:T(8,128)}, u32[]{:S(2)}) copy-start(f32[32,2048]{1,0:T(8,128)} %param.8) | copy-start | bytes 786436
  73.8 2.1 %copy-start.1 = (bf16[256,2048]{1,0:T(8,128)(2,1)S(1)}, bf16[256,2048]{1,0:T(8,128)(2,1)}, u32[]{:S(2)}) copy-start(bf16[256,2048]{1,0:T(8,128)(2,1)} %get-tuple-element.18) | copy-start | bytes 3145732

commit v3 on v2

--- a/solution.py
+++ b/solution.py
@@ -123,15 +123,12 @@
         cp.start()
     loads[0].wait()
     wone(x, zl, y, core)[...] = t_v[...].astype(BF)
-    loads[1].wait()
 
     def turn(ll):
-        for j in (2 * ll, 2 * ll + 1):
-            pt[ll, pl.ds((j % 2) * 4, 4), :, my_tok] = (
-                p_v[:, j * 256:(j + 1) * 256].T.reshape(4, 64, TOK)
-            )
-
-    turn(0)
+        for j in range(2):
+            cols = pl.ds(pl.multiple_of(ll * 512 + j * 256, 256), 256)
+            pt[ll, pl.ds(j * 4, 4), :, my_tok] = p_v[:, cols].T.reshape(4, 64, TOK)
+
     pl.semaphore_wait(barrier, len(partners))
 
     r_c = new_recv()
@@ -140,10 +137,11 @@
     for r, d in zip(r_z, (1, -1, 2)):
         send(wone(x, zl, y, core), wone(x, zl, y, core), r, at_z(d))
     send(c_ref.at[:, pl.ds(pl.multiple_of(other * HALF, HALF), HALF)], cc.at[my_tok, :], r_c, sister)
-    for ll in range(NL):
-        if ll:
-            turn(ll)
-        send(pt.at[ll, :, :, my_tok], pt.at[ll, :, :, my_tok], r_p[ll], sister)
+    groups = [lax.rem(zl + k, NL) for k in (0, 1, 3, 2)]
+    loads[1].wait()
+    for k, ll in enumerate(groups):
+        turn(ll)
+        send(pt.at[ll, :, :, my_tok], pt.at[ll, :, :, my_tok], r_p[k], sister)
     loads[2].wait()
 
     for r, d in zip(r_z, (1, -1, 2)):
@@ -269,12 +267,12 @@
 
     r_da, r_db = new_recv(), new_recv()
     def direct_a():
-        for d in range(1, NZ):
+        for d in (4, 3, 5, 2, 6, 1, 7):
             zz = lax.rem(z + d, NZ)
             send(sum_a.at[lax.rem(zz, NL), zz // NL], got_a.at[d - 1], r_da, at_z(d))
 
     def direct_b():
-        for d in range(1, NY):
+        for d in (4, 3, 5, 2, 6, 1, 7):
             send(sum_b.at[lax.rem(y + d, NY)], got_b.at[d - 1], r_db, at_y(d))
 
     r_x = {part: [new_recv() for _ in range(3)] for part in "ab"}
@@ -288,7 +286,7 @@
         for k in range(7):
             value = value + got[k].astype(F32)
         four[x] = value.astype(BF)
-        for d in range(1, NX):
+        for d in (2, 1, 3):
             send(four.at[x], four.at[x], r_x[part][d - 1], at_x(d))
 
     def quad(part):
@@ -332,16 +330,18 @@
 
     y_own()
     wait(cc.at[ot_tok, :], r_c)
-    for ll in range(NL):
-        wait(pt.at[ll, :, :, ot_tok], r_p[ll])
+    wait(pt.at[groups[0], :, :, ot_tok], r_p[0])
+    ring_step("b", 0, 1)
+    ring_step("b", 1, 1)
+    wait(pt.at[groups[1], :, :, ot_tok], r_p[1])
+    ring_step("b", 3, 1)
+    wait(pt.at[groups[2], :, :, ot_tok], r_p[2])
+    ring_step("b", 2, 1)
+    wait(pt.at[groups[3], :, :, ot_tok], r_p[3])
     ring_step("a", 0, 1)
     ring_step("a", 1, 1)
-    ring_step("b", 1, 1)
     y_from(0, 1)
-    ring_step("b", 0, 1)
     ring_step("a", 3, 1)
-    ring_step("b", 3, 1)
-    ring_step("b", 2, 1)
     ring_step("a", 0, 2)
     y_from(1, 1)
     ring_step("b", 1, 2)

time: 77 us -> 75.8 us (0.984)
  Pallas kernels: 73 us -> 71.8 us
    pallas_call x1, Pallas kernels: 73 us -> 71.8 us  [per_device(): pl.pallas_call(kernel, out_shape=(jax.ShapeDtypeStruct((TOK, FEAT), BF),...]
where the time goes in v3:
time: 75.8 us; the launch traced here: 75.6 us
  Pallas kernels  71.8 us (95%)
  other arithmetic  2.1 us (3%)
  local copies, waits for them, and re-layouts  0.99 us (1%)
    pallas_call x1, Pallas kernels, per_device(): pl.pallas_call(kernel, out_shape=(jax.ShapeDtypeStruct((TOK, FEAT), BF),...  71.8 us
    add x1, other arithmetic, update_shard(): new_teacher = ema_keep * teacher + (1.0 - ema_keep) * new_student  2.1 us

profile of v3, /device:TPU:1, one launch (start us, length us, event | category | flops | bytes accessed | tf_op | source)
XLA Modules:
  0.0 75.6 jit_solution(13313161801451414808)
XLA Ops:
  0.6 0.0 copy-start
  0.6 0.0 copy-start.4
  0.7 0.0 copy-start.3
  0.7 0.0 copy-start.2
  0.7 71.8 %shard_map.101 = (bf16[256,2048]{1,0:T(8,128)(2,1)}, bf16[32,2048]{1,0:T(8,128)(2,1)}) custom-call(bf16[256,2048]{1,0:T(8,128)(2,1)} %p_ref.1, bf16[256,2048]{1,0:T(8,128)(2,1)} %c_ref.1, f32[32,2048]{1,0:T(8,128)} %t_ref.1), custom_call_target="tpu_custom_call" | custom-call | tf_op jit(solution)/shard_map/pallas_call | solution.py:421
  72.5 0.0 copy-done
  72.5 0.0 copy-done.4
  72.5 0.0 copy-done.3
  72.5 0.0 copy-done.2
  72.5 0.0 copy-start.1
  72.6 2.1 %multiply_add_fusion = (f32[32,2048]{1,0:T(8,128)}, f32[32,2048]{1,0:T(8,128)}, f32[32,2048]{1,0:T(8,128)}, f32[32,2048]{1,0:T(8,128)}) fusion(f32[32,2048]{1,0:T(8,128)S(1)} %copy-done, f32[32,2048]{1,0:T(8,128)S(1)} %copy-done.2, bf16[32,2048]{1,0:T(8,128)(2,1)} %get-tuple-element.8, f32[32,2048]{1,0:T(8,128)S(1)} %copy-done.3, f32[32,2048]{1,0:T(8,128)S(1)} %copy-done.4), kind=kLoop, calls=%fused_computation.4 | loop fusion | flops 1245184 | bytes 2228224 | tf_op jit(solution)/shard_map/add | solution.py:39
  74.7 0.0 copy-done.1
  74.7 1.0 %copy.12 = bf16[256,2048]{1,0:T(8,128)(2,1)} copy(bf16[256,2048]{1,0:T(8,128)(2,1)S(1)} %copy-done.1) | data formatting | bytes 2097152
Async XLA Ops:
  0.6 71.9 %copy-start = (f32[32,2048]{1,0:T(8,128)S(1)}, f32[32,2048]{1,0:T(8,128)}, u32[]{:S(2)}) copy-start(f32[32,2048]{1,0:T(8,128)} %t_ref.1) | copy-start | bytes 786436
  0.6 71.9 %copy-start.4 = (f32[32,2048]{1,0:T(8,128)S(1)}, f32[32,2048]{1,0:T(8,128)}, u32[]{:S(2)}) copy-start(f32[32,2048]{1,0:T(8,128)} %param.10) | copy-start | bytes 786436
  0.7 71.9 %copy-start.3 = (f32[32,2048]{1,0:T(8,128)S(1)}, f32[32,2048]{1,0:T(8,128)}, u32[]{:S(2)}) copy-start(f32[32,2048]{1,0:T(8,128)} %param.9) | copy-start | bytes 786436
  0.7 71.9 %copy-start.2 = (f32[32,2048]{1,0:T(8,128)S(1)}, f32[32,2048]{1,0:T(8,128)}, u32[]{:S(2)}) copy-start(f32[32,2048]{1,0:T(8,128)} %param.8) | copy-start | bytes 786436
  72.5 2.1 %copy-start.1 = (bf16[256,2048]{1,0:T(8,128)(2,1)S(1)}, bf16[256,2048]{1,0:T(8,128)(2,1)}, u32[]{:S(2)}) copy-start(bf16[256,2048]{1,0:T(8,128)(2,1)} %get-tuple-element.18) | copy-start | bytes 3145732
